TPU v7x, 128 devices: a whole 4x4x4 slice. The times are simulated.
128 devices in a mesh: row: 8 (over z_lo, y), col: 16 (over x, z_hi, core).
Axes of the slice: x: 4, y: 4, z: 4 (z_hi: 2, z_lo: 2; z = z_hi * 2 + z_lo), core: 2. Of those that a mesh axis runs over, the one named last changes fastest.
Arguments:
- amplitudes: bfloat16 [12288, 8192], P('row', 'col'), may hold values from -6 to 6
- integrals: bfloat16 [8192, 8192], P('row', 'col'), may hold values from -0.09375 to 0.09375
- screen_mask: int32 [96, 64], P('row', 'col'), may hold values from 0 to 1, as said below
- tile_order: int32 [64], replicated, may hold values from 0 to 63, each once
Outputs:
- ladder: float32 [12288, 8192], P('row', 'col')
Inputs may be any that keep to these rules, and one draw needn't show every extreme that they name: `screen_mask`: in every aligned block of 12 tile rows by 4 tile columns exactly 24 tiles survive; rows of tiles hold different numbers of them. `tile_order`: each number of 0 to 63 appears once.
All inputs are finite; a program needn't handle non-finite values.
Results may differ from a plain program's by a relative error of at most 0.0003.
Values may be sent and summed in bfloat16 or wider, within the bound.
A program may use at most 256 MiB of HBM per device.

v0:
```python
import jax
import jax.numpy as jnp
from jax import lax
from jax.sharding import PartitionSpec as P

TILE_PAIRS = 128


def accumulate(left, right):
    return jnp.dot(left, right, preferred_element_type=jnp.float32)


def ordered_rows(integrals, tile_order):
    result_cols = integrals.shape[1]
    all_tiles = tile_order.shape[0]
    gathered = lax.all_gather(integrals, "row", axis=0, tiled=True)
    return jnp.take(
        gathered.reshape(all_tiles, TILE_PAIRS, result_cols), tile_order, axis=0
    ).reshape(all_tiles * TILE_PAIRS, result_cols)


def local(amplitudes, integrals, screen_mask, tile_order):
    local_rows = amplitudes.shape[0]
    local_cols = amplitudes.shape[1]
    row_tiles = local_rows // TILE_PAIRS
    col_tiles = local_cols // TILE_PAIRS
    weight_values = screen_mask.astype(jnp.bfloat16)[:, None, :, None]
    screened_tiles = (
        amplitudes.reshape(row_tiles, TILE_PAIRS, col_tiles, TILE_PAIRS) * weight_values
    ).reshape(local_rows, local_cols)
    ordered = ordered_rows(integrals, tile_order)
    return accumulate(lax.all_gather(screened_tiles, "col", axis=1, tiled=True), ordered)


def solution(mesh):
    placed = (P("row", "col"), P("row", "col"), P("row", "col"), P())
    return jax.shard_map(
        local, mesh=mesh, in_specs=placed, out_specs=P("row", "col"), check_vma=False
    )
```

profile of v0, /device:TPU:1, one launch (start us, length us, event | category | flops | bytes accessed | tf_op | source)
XLA Modules:
  0.0 299.6 jit_solution(6476799659595372149)
XLA Ops:
  6.5 0.0 copy-start
  6.5 0.0 all-gather.5.cloned.1.call-start
  6.5 0.7 all-gather.5.cloned.1.call-update
  7.3 0.0 all-gather.3.cloned.1.call-start
  7.3 0.7 convert_element_type.3
  8.0 0.1 copy.5
  8.1 0.5 mul.11
  8.6 2.8 bitcast_multiply_fusion
  11.3 0.0 all-gather.3.cloned.1.call-update
  11.4 0.0 copy-done
  11.4 0.1 broadcast_bitcast_fusion
  11.5 92.7 %all-gather.5.cloned.1.call-done = bf16[8192,512]{1,0:T(8,128)(2,1)} async-done(((bf16[1024,512]{1,0:T(8,128)(2,1)}), bf16[8192,512]{1,0:T(8,128)(2,1)}) %all-gather.5.cloned.1.call-update) | async-done | bytes 8388624 | tf_op jit(solution)/shard_map/all_gather | solution.py:16
  104.2 8.9 %gather_fusion = bf16[64,128,512]{2,1,0:T(8,128)(2,1)} fusion(bf16[64,128,512]{2,1,0:T(8,128)(2,1)} %bitcast.11, s32[1024]{0:T(1024)S(1)} %pad_clamp_fusion), kind=kCustom, calls=%fused_computation | custom fusion | bytes 16777472 | tf_op jit(solution)/shard_map/jit(_take)/gather | solution.py:17
  113.2 7.8 %bitcast_select_fusion = bf16[8192,512]{1,0:T(8,128)(2,1)} fusion(bf16[64,128,512]{2,1,0:T(8,128)(2,1)} %gather_fusion, pred[8192]{0:T(1024)(128)(4,1)S(1)} %broadcast_bitcast_fusion), kind=kLoop, calls=%fused_computation.1 | loop fusion | flops 4194304 | bytes 16785408 | tf_op jit(solution)/shard_map/jit(_take)/select_n | solution.py:17
  120.9 151.6 %all-gather.3.cloned.1.call-done = bf16[1536,8192]{1,0:T(8,128)(2,1)} async-done(((bf16[1536,512]{1,0:T(8,128)(2,1)}), bf16[1536,8192]{1,0:T(8,128)(2,1)}) %all-gather.3.cloned.1.call-update) | async-done | bytes 25165840 | tf_op jit(solution)/shard_map/all_gather | solution.py:32
  272.5 20.2 %fusion = f32[1536,512]{1,0:T(8,128)} fusion(bf16[1536,8192]{1,0:T(8,128)(2,1)} %all-gather.3.cloned.1.call-done, bf16[8192,512]{1,0:T(8,128)(2,1)} %bitcast_select_fusion), kind=kOutput, calls=%fused_computation.7 | convolution fusion | flops 12884901888 | bytes 36700160 | tf_op jit(solution)/shard_map/dot_general | solution.py:10
  (3 shorter events, 0.0 us)
Async XLA Ops:
  6.5 4.8 %copy-start = (s32[64]{0:T(128)S(1)}, s32[64]{0:T(128)}, u32[]{:S(2)}) copy-start(s32[64]{0:T(128)} %param.7) | copy-start | bytes 772
  6.5 97.7 %all-gather.5.cloned.1.call-start = ((), (), s32[]{:S(2)}) async-start(), calls=%async_computation.1 | async-start | bytes 9437184 | tf_op jit(solution)/shard_map/all_gather | solution.py:16
  7.3 265.3 %all-gather.3.cloned.1.call-start = ((), (), s32[]{:S(2)}) async-start(), calls=%async_computation | async-start | bytes 26738688 | tf_op jit(solution)/shard_map/all_gather | solution.py:32
Sparse Core Ops, SparseCore 0:
  9.0 95.1 all-gather.4
  106.5 165.9 all-gather.2
where the time goes:
time: 300 us
  waiting for transfers between devices  245 us (82%)
  matrix products  20.2 us (7%)
  between operations  13.4 us (4%)
  other arithmetic  11.2 us (4%)
  local copies, waits for them, and re-layouts  9.57 us (3%)
    all_gather x1, waiting for transfers between devices, local(): lax.all_gather(screened_tiles, 'col', axis=1, tiled=True)  152 us
    all_gather x1, waiting for transfers between devices, ordered_rows(): gathered = lax.all_gather(integrals, 'row', axis=0, tiled=True)  92.7 us
    dot_general x1, matrix products, accumulate(): return jnp.dot(left, right, preferred_element_type=jnp.float32)  20.2 us
    gather x1, local copies, waits for them, and re-layouts, ordered_rows(): jnp.take(gathered.reshape(all_tiles, TILE_PAIRS, result_cols), tile_order...  8.91 us
    select_n x2, other arithmetic, ordered_rows(): jnp.take(gathered.reshape(all_tiles, TILE_PAIRS, result_cols), tile_order...  7.77 us
  transfers between devices with their start and end apart: 2, of which 2 were waited for; matrix products, arithmetic and copies ran while one was open for 7% of the time, Pallas kernels for 0%

commit v1 on v0

v1 whole, which is shorter than its diff:
```python
import jax
import jax.numpy as jnp
from jax import lax
from jax.experimental import pallas as pl
from jax.experimental.pallas import tpu as pltpu
from jax.sharding import PartitionSpec as P

MESH = pl.DeviceIdType.MESH
T = 128
ROWT, KT, CAP = 12, 4, 24
M = ROWT * T
DEPTH = 8
H = 256
ZERO = CAP
CUT = 5
CHUNK = 768

B_IDS = ("zp", "yp", "ym", "pp", "pm", "fp", "fm", "zhp", "zhm", "gp", "gm")
A_IDS = ("ax+", "ax-", "az", "ac", "bx+", "bx-", "bc", "af+", "af-", "bf+", "bf-",
         "c1", "c2", "c3", "d1", "d2", "d3")
IDS = {}
for _h in (0, 1):
    for _n in B_IDS:
        IDS[(_n, _h)] = len(IDS)
for _n in A_IDS:
    IDS[_n] = len(IDS)
for _n in A_IDS:
    if _n not in ("af-", "bf-"):
        IDS[("m", _n)] = len(IDS)


def kernel(a_in, b_in, mask, order, out, *scratch):
    A = scratch[0:16]
    meta = scratch[16:32]
    (a_loc, dense, b0, b1, acc0, acc1, inv_v, inv_s, nxt, pos, cnt, ss, rs, ls) = scratch[32:]
    B, ACC = (b0, b1), (acc0, acc1)
    row, col = lax.axis_index("row"), lax.axis_index("col")
    y, zl = lax.rem(row, 4), lax.div(row, 4)
    core, zh, x = lax.rem(col, 2), lax.rem(lax.div(col, 2), 2), lax.div(col, 4)

    def at(dx=0, dy=0, dzl=0, dzh=0, dcore=0):
        r = lax.rem(zl + dzl, 2) * 4 + lax.rem(y + dy, 4)
        c = (lax.rem(x + dx, 4) * 2 + lax.rem(zh + dzh, 2)) * 2 + lax.rem(core + dcore, 2)
        return r, c

    up, down, zpart = at(dy=1), at(dy=3), at(dzl=1)
    right, left, hpart, sib = at(dx=1), at(dx=3), at(dzh=1), at(dcore=1)
    peers = (up, down, zpart, right, left, hpart, sib)

    barrier = pltpu.get_barrier_semaphore()
    for p in peers:
        pl.semaphore_signal(barrier, inc=1, device_id=p, device_id_type=MESH)

    local = []
    for k in range(KT):
        local.append(pltpu.make_async_copy(a_in.at[:, :, pl.ds(k * T, T)], a_loc.at[pl.ds(k * ROWT, ROWT)], ls.at[k]))
    for h in (0, 1):
        local.append(pltpu.make_async_copy(b_in.at[:, :, pl.ds(h * H, H)], B[h].at[pl.ds(row * DEPTH, DEPTH)], ls.at[KT + h]))
    for c in local:
        c.start()
    pl.semaphore_wait(barrier, len(peers))

    started = []

    def send(name, src, dst, device):
        i = IDS[name]
        c = pltpu.make_async_remote_copy(src, dst, ss.at[i], rs.at[i], device_id=device, device_id_type=MESH)
        c.start()
        started.append(c)

    def got(name, ref):
        i = IDS[name]
        pltpu.make_async_remote_copy(ref, ref, ss.at[i], rs.at[i], device_id=sib, device_id_type=MESH).wait_recv()

    def rows_of(h, dzl, dy, first=0, count=DEPTH):
        r = lax.rem(zl + dzl, 2) * 4 + lax.rem(y + dy, 4)
        return B[h].at[pl.ds(r * DEPTH + first, count)]

    def b_send(name, h, dzl, dy, device, first=0, count=DEPTH, own=False):
        dst = rows_of(h, dzl, dy, first, count)
        src = b_in.at[:, :, pl.ds(h * H, H)] if own else dst
        send((name, h), src, dst, device)

    HALF = DEPTH // 2
    LANDS = {
        "zp": (1, 0, 0, DEPTH), "yp": (0, 3, 0, DEPTH), "ym": (0, 1, 0, DEPTH),
        "pp": (1, 3, 0, CUT), "pm": (1, 1, DEPTH - CUT, CUT),
        "fp": (0, 2, 0, HALF), "fm": (0, 2, HALF, HALF),
        "zhp": (1, 3, CUT, DEPTH - CUT), "zhm": (1, 1, 0, DEPTH - CUT),
        "gp": (1, 2, 0, HALF), "gm": (1, 2, HALF, HALF),
    }

    def b_got(h, *names):
        for n in names:
            got((n, h), rows_of(h, *LANDS[n]))

    def b_own_y(h):
        b_send("yp", h, 0, 0, up, own=True)
        b_send("ym", h, 0, 0, down, own=True)

    def b_own_z(h):
        b_send("zp", h, 0, 0, zpart, own=True)

    def b_near(h):
        b_got(h, "yp")
        b_send("fp", h, 0, 3, up, 0, HALF)
        b_got(h, "ym")
        b_send("fm", h, 0, 1, down, HALF, HALF)
        b_send("zhp", h, 0, 3, zpart, CUT, DEPTH - CUT)
        b_send("zhm", h, 0, 1, zpart, 0, DEPTH - CUT)

    def b_partner(h):
        b_got(h, "zp")
        b_send("pp", h, 1, 0, up, 0, CUT)
        b_send("pm", h, 1, 0, down, DEPTH - CUT, CUT)

    def b_far(h):
        b_got(h, "pp")
        b_send("gp", h, 1, 3, up, 0, HALF)
        b_got(h, "pm")
        b_send("gm", h, 1, 1, down, HALF, HALF)

    def slot(dzh, dcore, dx):
        return dzh * 8 + dcore * 4 + dx

    A_LANDS = {
        "ax+": (slot(0, 0, 3), 0, CAP), "ax-": (slot(0, 0, 1), 0, CAP),
        "az": (slot(1, 0, 0), 0, CAP), "ac": (slot(0, 1, 0), 0, CAP),
        "bx+": (slot(1, 0, 3), 0, CAP), "bx-": (slot(1, 0, 1), 0, CAP), "bc": (slot(1, 1, 0), 0, CAP),
        "af+": (slot(0, 0, 2), 0, CAP // 2), "af-": (slot(0, 0, 2), CAP // 2, CAP // 2),
        "bf+": (slot(1, 0, 2), 0, CAP // 2), "bf-": (slot(1, 0, 2), CAP // 2, CAP // 2),
        "c1": (slot(0, 1, 1), 0, CAP), "c2": (slot(0, 1, 2), 0, CAP), "c3": (slot(0, 1, 3), 0, CAP),
        "d1": (slot(1, 1, 1), 0, CAP), "d2": (slot(1, 1, 2), 0, CAP), "d3": (slot(1, 1, 3), 0, CAP),
    }

    def a_send(name, src, device):
        s, first, count = A_LANDS[name]
        rows = pl.ds(first, count)
        send(name, A[src].at[rows], A[s].at[rows], device)
        if ("m", name) in IDS:
            send(("m", name), meta[src], meta[s], device)

    def a_got(*names):
        for n in names:
            s, first, count = A_LANDS[n]
            got(n, A[s].at[pl.ds(first, count)])
            if ("m", n) in IDS:
                got(("m", n), meta[s])

    def col_of(g):
        dzh, dcore, dx = lax.div(g, 8), lax.rem(lax.div(g, 4), 2), lax.rem(g, 4)
        return (lax.rem(x + dx, 4) * 2 + lax.rem(zh + dzh, 2)) * 2 + lax.rem(core + dcore, 2)

    def expand(s):
        base = col_of(jnp.int32(s)) * KT

        @pl.loop(0, KT * ROWT)
        def _(t):
            rows = pl.ds(pl.multiple_of(lax.rem(t, ROWT) * T, T), T)
            dense[base + lax.div(t, ROWT), rows, :] = A[s][meta[s][t]]

    def left_part(g):
        c = col_of(g)
        for m in range(M // CHUNK):
            lhs = jnp.concatenate(
                [dense[c * KT + j, pl.ds(m * CHUNK, CHUNK), :] for j in range(KT)], axis=1)
            rhs = jnp.concatenate(
                [b0[order[c * KT + j]] for j in range(KT)], axis=0)
            acc0[pl.ds(m * CHUNK, CHUNK), :] += jnp.dot(lhs, rhs, preferred_element_type=jnp.float32)

    def right_part(g):
        r = lax.rem(zl + lax.div(g, 4), 2) * 4 + lax.rem(y + lax.rem(g, 4), 4)
        for m in range(M // CHUNK):
            for q in (0, 1):
                lhs = jnp.concatenate(
                    [dense[inv_s[0, r * 8 + q * 4 + j], pl.ds(m * CHUNK, CHUNK), :]
                     for j in range(4)], axis=1)
                rhs = b1[pl.ds(r * DEPTH + q * 4, 4)].reshape(4 * T, H)
                acc1[pl.ds(m * CHUNK, CHUNK), :] += jnp.dot(lhs, rhs, preferred_element_type=jnp.float32)

    b_own_y(0)
    b_own_z(0)

    nxt[KT * ROWT] = 0

    @pl.loop(0, KT * ROWT)
    def _(n):
        t = KT * ROWT - 1 - n
        keep = mask[lax.rem(t, ROWT), lax.div(t, ROWT)]
        nxt[t] = keep * t + (1 - keep) * nxt[t + 1]

    cnt[0] = 0

    @pl.loop(0, KT * ROWT)
    def _(t):
        keep = mask[lax.rem(t, ROWT), lax.div(t, ROWT)]
        meta[0][t] = keep * cnt[t] + (1 - keep) * ZERO
        cnt[t + 1] = cnt[t] + keep

    for k in range(KT):
        local[k].wait()
    pos[0] = nxt[0]

    @pl.loop(0, CAP)
    def _(s):
        A[0][s] = a_loc[pos[s]]
        pos[s + 1] = nxt[pos[s] + 1]

    a_send("ax+", 0, right)
    a_send("ax-", 0, left)
    a_send("az", 0, hpart)
    a_send("ac", 0, sib)

    lane = lax.broadcasted_iota(jnp.int32, (8, 128), 1)
    inv_v[...] = jnp.zeros((8, 128), jnp.int32)

    @pl.loop(0, 64)
    def _(k):
        apart = lane - order[k]
        inv_v[...] += (k - inv_v[...]) * (1 - jnp.minimum(jnp.maximum(apart, -apart), 1))

    to_s = pltpu.make_async_copy(inv_v, inv_s, ls.at[KT + 2])
    to_s.start()
    for s in range(16):
        A[s][ZERO] = jnp.zeros((T, T), jnp.bfloat16)
    acc0[...] = jnp.zeros_like(acc0)
    acc1[...] = jnp.zeros_like(acc1)
    expand(0)
    to_s.wait()
    local[KT].wait()
    local[KT + 1].wait()

    b_near(0)
    b_own_y(1)
    a_got("ac")
    expand(slot(0, 1, 0))
    a_got("ax+")
    a_send("af+", slot(0, 0, 3), right)
    a_send("c3", slot(0, 0, 3), sib)
    a_got("ax-")
    a_send("af-", slot(0, 0, 1), left)
    a_send("c1", slot(0, 0, 1), sib)
    expand(slot(0, 0, 3))
    expand(slot(0, 0, 1))
    b_partner(0)
    b_own_z(1)
    a_got("az")
    a_send("bx+", slot(1, 0, 0), right)
    a_send("bx-", slot(1, 0, 0), left)
    a_send("bc", slot(1, 0, 0), sib)
    b_near(1)
    a_got("af+", "af-")
    a_send("c2", slot(0, 0, 2), sib)
    expand(slot(1, 0, 0))
    expand(slot(0, 0, 2))
    for n in ("c1", "c3", "c2"):
        a_got(n)
        expand(A_LANDS[n][0])
    b_far(0)
    b_partner(1)
    a_got("bx+")
    a_send("bf+", slot(1, 0, 3), right)
    a_send("d3", slot(1, 0, 3), sib)
    a_got("bx-")
    a_send("bf-", slot(1, 0, 1), left)
    a_send("d1", slot(1, 0, 1), sib)
    expand(slot(1, 0, 3))
    expand(slot(1, 0, 1))
    a_got("bc")
    expand(slot(1, 1, 0))
    b_got(0, "fp", "fm", "zhp", "zhm", "gp", "gm")
    pl.loop(0, 4)(left_part)
    b_far(1)
    pl.loop(4, 8)(left_part)
    a_got("bf+", "bf-")
    a_send("d2", slot(1, 0, 2), sib)
    expand(slot(1, 0, 2))
    for n in ("d1", "d3", "d2"):
        a_got(n)
        expand(A_LANDS[n][0])
    pl.loop(8, 16)(left_part)
    left_out = pltpu.make_async_copy(acc0, out.at[:, pl.ds(0, H)], ls.at[0])
    left_out.start()
    b_got(1, "fp", "fm")
    pl.loop(0, 5)(right_part)
    b_got(1, "zhp", "zhm")
    right_part(jnp.int32(5))
    right_part(jnp.int32(7))
    b_got(1, "gp", "gm")
    right_part(jnp.int32(6))
    right_out = pltpu.make_async_copy(acc1, out.at[:, pl.ds(H, H)], ls.at[1])
    right_out.start()
    for c in started:
        c.wait_send()
    left_out.wait()
    right_out.wait()


def local_step(amplitudes, integrals, screen_mask, tile_order):
    n = len(IDS)
    scratch = [pltpu.VMEM((CAP + 1, T, T), jnp.bfloat16)] * 16 + [pltpu.SMEM((64,), jnp.int32)] * 16
    scratch += [
        pltpu.VMEM((KT * ROWT, T, T), jnp.bfloat16),
        pltpu.VMEM((64, M, T), jnp.bfloat16),
        pltpu.VMEM((8 * DEPTH, T, H), jnp.bfloat16),
        pltpu.VMEM((8 * DEPTH, T, H), jnp.bfloat16),
        pltpu.VMEM((M, H), jnp.float32),
        pltpu.VMEM((M, H), jnp.float32),
        pltpu.VMEM((8, 128), jnp.int32),
        pltpu.SMEM((8, 128), jnp.int32),
        pltpu.SMEM((KT * ROWT + 2,), jnp.int32),
        pltpu.SMEM((KT * ROWT + 2,), jnp.int32),
        pltpu.SMEM((KT * ROWT + 2,), jnp.int32),
        pltpu.SemaphoreType.DMA((n,)),
        pltpu.SemaphoreType.DMA((n,)),
        pltpu.SemaphoreType.DMA((KT + 3,)),
    ]
    anywhere = pl.BlockSpec(memory_space=pl.ANY)
    scalars = pl.BlockSpec(memory_space=pltpu.SMEM)
    return pl.pallas_call(
        kernel,
        out_shape=jax.ShapeDtypeStruct((M, 2 * H), jnp.float32),
        in_specs=[anywhere, anywhere, scalars, scalars],
        out_specs=anywhere,
        scratch_shapes=scratch,
        cost_estimate=pl.CostEstimate(flops=2 * M * 512 * 8192, bytes_accessed=6 << 20, transcendentals=0),
        compiler_params=pltpu.CompilerParams(
            collective_id=0, has_side_effects=True, vmem_limit_bytes=58 << 20
        ),
    )(amplitudes.reshape(ROWT, T, KT * T), integrals.reshape(DEPTH, T, 2 * H), screen_mask, tile_order)


def solution(mesh):
    placed = (P("row", "col"), P("row", "col"), P("row", "col"), P())
    return jax.shard_map(
        local_step, mesh=mesh, in_specs=placed, out_specs=P("row", "col"), check_vma=False
    )
```

time: 300 us -> 91.6 us (0.31)
  waiting for transfers between devices: 245 us -> 0 us
  Pallas kernels: 0 us -> 86.2 us
  matrix products: 20.2 us -> 0 us
  between operations: 13.4 us -> 0.01 us
  other arithmetic: 11.2 us -> 0 us
  local copies, waits for them, and re-layouts: 9.57 us -> 5.22 us
    all_gather x2 -> x0, waiting for transfers between devices: 244 us -> none  [the longest x1 152 us: local(): lax.all_gather(screened_tiles, 'col', axis=1, tiled=True)]
    pallas_call x0 -> x1, Pallas kernels: none -> 86.2 us  [local_step(): pl.pallas_call(kernel, out_shape=jax.ShapeDtypeStruct((M, 2 * H), jnp.flo...]
    dot_general x1 -> x0, matrix products: 20.2 us -> none  [accumulate(): return jnp.dot(left, right, preferred_element_type=jnp.float32)]
    gather x1 -> x0, local copies, waits for them, and re-layouts: 8.91 us -> none  [ordered_rows(): jnp.take(gathered.reshape(all_tiles, TILE_PAIRS, result_cols), tile_order...]
    select_n x2 -> x0, other arithmetic: 7.77 us -> none  [ordered_rows(): jnp.take(gathered.reshape(all_tiles, TILE_PAIRS, result_cols), tile_order...]
    unnamed x2, local copies, waits for them, and re-layouts: 0.01 us -> 5.22 us
  transfers between devices with their start and end apart: 2 -> 0, of which waited for: 2 -> 0; matrix products, arithmetic and copies ran while one was open for 7% -> 0% of each run, Pallas kernels for 0% -> 0%
where the time goes in v1:
time: 91.6 us; the launch traced here: 91.4 us
  Pallas kernels  86.2 us (94%)
  local copies, waits for them, and re-layouts  5.22 us (6%)
    pallas_call x1, Pallas kernels, local_step(): pl.pallas_call(kernel, out_shape=jax.ShapeDtypeStruct((M, 2 * H), jnp.flo...  86.2 us
    unnamed x2, local copies, waits for them, and re-layouts  5.22 us

profile of v1, /device:TPU:1, one launch (start us, length us, event | category | flops | bytes accessed | tf_op | source)
XLA Modules:
  0.0 91.4 jit_solution(12178244261730409975)
XLA Ops:
  0.0 1.4 %copy.5.mask = s32[12,4]{1,0:T(8,128)} copy(s32[12,4]{0,1:T(4,128)} %param.6) | data formatting | bytes 384 | tf_op args[2]
  1.4 86.2 %shard_map.46 = f32[1536,512]{1,0:T(8,128)} custom-call(bf16[12,128,512]{2,1,0:T(8,128)(2,1)} %bitcast.2, bf16[8,128,512]{2,1,0:T(8,128)(2,1)} %bitcast.3, s32[12,4]{1,0:T(8,128)} %copy.5.mask, s32[64]{0:T(128)} %order.1), custom_call_target="tpu_custom_call" | custom-call | flops 12884901888 | bytes 6291456 | tf_op jit(solution)/shard_map/pallas_call | solution.py:320
  87.6 3.9 %copy.7 = f32[1536,512]{1,0:T(8,128)} copy(f32[1536,512]{1,0:T(8,128)} %shard_map.46) | data formatting | bytes 6291456

commit v2 on v1

--- a/solution.py
+++ b/solution.py
@@ -32,8 +32,8 @@
 def kernel(a_in, b_in, mask, order, out, *scratch):
     A = scratch[0:16]
     meta = scratch[16:32]
-    (a_loc, dense, b0, b1, acc0, acc1, inv_v, inv_s, nxt, pos, cnt, ss, rs, ls) = scratch[32:]
-    B, ACC = (b0, b1), (acc0, acc1)
+    (a_loc, dense, b0, b1, inv_v, inv_s, nxt, pos, cnt, ss, rs, ls) = scratch[32:]
+    B = (b0, b1)
     row, col = lax.axis_index("row"), lax.axis_index("col")
     y, zl = lax.rem(row, 4), lax.div(row, 4)
     core, zh, x = lax.rem(col, 2), lax.rem(lax.div(col, 2), 2), lax.div(col, 4)
@@ -166,7 +166,7 @@
                 [dense[c * KT + j, pl.ds(m * CHUNK, CHUNK), :] for j in range(KT)], axis=1)
             rhs = jnp.concatenate(
                 [b0[order[c * KT + j]] for j in range(KT)], axis=0)
-            acc0[pl.ds(m * CHUNK, CHUNK), :] += jnp.dot(lhs, rhs, preferred_element_type=jnp.float32)
+            out[pl.ds(m * CHUNK, CHUNK), pl.ds(0, H)] += jnp.dot(lhs, rhs, preferred_element_type=jnp.float32)
 
     def right_part(g):
         r = lax.rem(zl + lax.div(g, 4), 2) * 4 + lax.rem(y + lax.rem(g, 4), 4)
@@ -176,7 +176,7 @@
                     [dense[inv_s[0, r * 8 + q * 4 + j], pl.ds(m * CHUNK, CHUNK), :]
                      for j in range(4)], axis=1)
                 rhs = b1[pl.ds(r * DEPTH + q * 4, 4)].reshape(4 * T, H)
-                acc1[pl.ds(m * CHUNK, CHUNK), :] += jnp.dot(lhs, rhs, preferred_element_type=jnp.float32)
+                out[pl.ds(m * CHUNK, CHUNK), pl.ds(H, H)] += jnp.dot(lhs, rhs, preferred_element_type=jnp.float32)
 
     b_own_y(0)
     b_own_z(0)
@@ -186,14 +186,14 @@
     @pl.loop(0, KT * ROWT)
     def _(n):
         t = KT * ROWT - 1 - n
-        keep = mask[lax.rem(t, ROWT), lax.div(t, ROWT)]
+        keep = mask[lax.div(t, ROWT), lax.rem(t, ROWT)]
         nxt[t] = keep * t + (1 - keep) * nxt[t + 1]
 
     cnt[0] = 0
 
     @pl.loop(0, KT * ROWT)
     def _(t):
-        keep = mask[lax.rem(t, ROWT), lax.div(t, ROWT)]
+        keep = mask[lax.div(t, ROWT), lax.rem(t, ROWT)]
         meta[0][t] = keep * cnt[t] + (1 - keep) * ZERO
         cnt[t + 1] = cnt[t] + keep
 
@@ -223,8 +223,7 @@
     to_s.start()
     for s in range(16):
         A[s][ZERO] = jnp.zeros((T, T), jnp.bfloat16)
-    acc0[...] = jnp.zeros_like(acc0)
-    acc1[...] = jnp.zeros_like(acc1)
+    out[...] = jnp.zeros_like(out)
     expand(0)
     to_s.wait()
     local[KT].wait()
@@ -279,8 +278,6 @@
         a_got(n)
         expand(A_LANDS[n][0])
     pl.loop(8, 16)(left_part)
-    left_out = pltpu.make_async_copy(acc0, out.at[:, pl.ds(0, H)], ls.at[0])
-    left_out.start()
     b_got(1, "fp", "fm")
     pl.loop(0, 5)(right_part)
     b_got(1, "zhp", "zhm")
@@ -288,12 +285,8 @@
     right_part(jnp.int32(7))
     b_got(1, "gp", "gm")
     right_part(jnp.int32(6))
-    right_out = pltpu.make_async_copy(acc1, out.at[:, pl.ds(H, H)], ls.at[1])
-    right_out.start()
     for c in started:
         c.wait_send()
-    left_out.wait()
-    right_out.wait()
 
 
 def local_step(amplitudes, integrals, screen_mask, tile_order):
@@ -304,8 +297,6 @@
         pltpu.VMEM((64, M, T), jnp.bfloat16),
         pltpu.VMEM((8 * DEPTH, T, H), jnp.bfloat16),
         pltpu.VMEM((8 * DEPTH, T, H), jnp.bfloat16),
-        pltpu.VMEM((M, H), jnp.float32),
-        pltpu.VMEM((M, H), jnp.float32),
         pltpu.VMEM((8, 128), jnp.int32),
         pltpu.SMEM((8, 128), jnp.int32),
         pltpu.SMEM((KT * ROWT + 2,), jnp.int32),
@@ -319,15 +310,15 @@
     scalars = pl.BlockSpec(memory_space=pltpu.SMEM)
     return pl.pallas_call(
         kernel,
-        out_shape=jax.ShapeDtypeStruct((M, 2 * H), jnp.float32),
+        out_shape=pltpu.VMEM((M, 2 * H), jnp.float32),
         in_specs=[anywhere, anywhere, scalars, scalars],
-        out_specs=anywhere,
+        out_specs=pl.BlockSpec(memory_space=pltpu.VMEM),
         scratch_shapes=scratch,
         cost_estimate=pl.CostEstimate(flops=2 * M * 512 * 8192, bytes_accessed=6 << 20, transcendentals=0),
         compiler_params=pltpu.CompilerParams(
             collective_id=0, has_side_effects=True, vmem_limit_bytes=58 << 20
         ),
-    )(amplitudes.reshape(ROWT, T, KT * T), integrals.reshape(DEPTH, T, 2 * H), screen_mask, tile_order)
+    )(amplitudes.reshape(ROWT, T, KT * T), integrals.reshape(DEPTH, T, 2 * H), screen_mask.T, tile_order)
 
 
 def solution(mesh):

time: 91.6 us -> 86.8 us (0.948)
  local copies, waits for them, and re-layouts: 5.22 us -> 1.67 us
  Pallas kernels: 86.2 us -> 85 us
    unnamed x2 -> x1, local copies, waits for them, and re-layouts: 5.22 us -> 1.67 us
    pallas_call x1, Pallas kernels: 86.2 us -> 85 us  [local_step(): pl.pallas_call(kernel, out_shape=pltpu.VMEM((M, 2 * H), jnp.float32), in_...]
where the time goes in v2:
time: 86.8 us; the launch traced here: 86.7 us
  Pallas kernels  85 us (98%)
  local copies, waits for them, and re-layouts  1.67 us (2%)
    pallas_call x1, Pallas kernels, local_step(): pl.pallas_call(kernel, out_shape=pltpu.VMEM((M, 2 * H), jnp.float32), in_...  85 us

profile of v2, /device:TPU:1, one launch (start us, length us, event | category | flops | bytes accessed | tf_op | source)
XLA Modules:
  0.0 86.7 jit_solution(10081403580853262784)
XLA Ops:
  0.0 85.0 %shard_map.46 = f32[1536,512]{1,0:T(8,128)S(1)} custom-call(bf16[12,128,512]{2,1,0:T(8,128)(2,1)} %bitcast.3, bf16[8,128,512]{2,1,0:T(8,128)(2,1)} %bitcast.4, s32[4,12]{1,0:T(4,128)} %bitcast.5, s32[64]{0:T(128)} %order.1), custom_call_target="tpu_custom_call" | custom-call | flops 12884901888 | bytes 6291456 | tf_op jit(solution)/shard_map/pallas_call | solution.py:311
  85.0 1.7 %copy.6 = f32[1536,512]{1,0:T(8,128)} copy(f32[1536,512]{1,0:T(8,128)S(1)} %shard_map.46) | data formatting | bytes 6291456

commit v3 on v0

v3 whole, which is shorter than its diff:
```python
import jax
import jax.numpy as jnp
from jax import lax
from jax.experimental import pallas as pl
from jax.experimental.pallas import tpu as pltpu
from jax.sharding import PartitionSpec as P

MESH = pl.DeviceIdType.MESH
T = 128
ROWT, KT, CAP = 12, 4, 24
M = ROWT * T
DEPTH = 8
H = 256
ZERO = CAP
CHUNK = 768

TRANSFERS = {
    "0U1": ("u", (0, 3), 0, 4),
    "0U2": ("u", (0, 3), 4, 4),
    "0D1": ("d", (0, 1), 4, 4),
    "0D2": ("d", (0, 1), 0, 4),
    "0Z1": ("z", (1, 0), 0, 4),
    "0Z2": ("z", (1, 0), 4, 4),
    "0FU": ("u", (0, 2), 0, 4),
    "0FD": ("d", (0, 2), 4, 4),
    "0PU1": ("u", (1, 3), 0, 4),
    "0PD1": ("d", (1, 1), 4, 4),
    "0PU2": ("u", (1, 3), 4, 2),
    "0PD2": ("d", (1, 1), 2, 2),
    "0ZU": ("z", (1, 3), 6, 2),
    "0ZD": ("z", (1, 1), 0, 2),
    "0GU": ("u", (1, 2), 0, 4),
    "0GD": ("d", (1, 2), 4, 4),
    "XR1": ("r", (0, 0, 3), 0, 12),
    "XR2": ("r", (0, 0, 3), 12, 12),
    "XL1": ("l", (0, 0, 1), 12, 12),
    "XL2": ("l", (0, 0, 1), 0, 12),
    "XFR": ("r", (0, 0, 2), 0, 12),
    "XFL": ("l", (0, 0, 2), 12, 12),
    "XS0": ("s", (0, 1, 0), 0, 24),
    "XS3": ("s", (0, 1, 3), 0, 24),
    "XS1": ("s", (0, 1, 1), 0, 24),
    "XT2": ("s", (0, 1, 2), 0, 12),
    "XU2": ("s", (0, 1, 2), 12, 12),
    "YR1": ("r", (1, 0, 3), 0, 12),
    "YR2": ("r", (1, 0, 3), 12, 12),
    "YL1": ("l", (1, 0, 1), 12, 12),
    "YL2": ("l", (1, 0, 1), 0, 12),
    "YFR": ("r", (1, 0, 2), 0, 12),
    "YFL": ("l", (1, 0, 2), 12, 12),
    "YS0": ("s", (1, 1, 0), 0, 24),
    "YS3": ("s", (1, 1, 3), 0, 24),
    "YS1": ("s", (1, 1, 1), 0, 24),
    "YT2": ("s", (1, 1, 2), 0, 12),
    "YU2": ("s", (1, 1, 2), 12, 12),
    "H1": ("z", (1, 0, 0), 0, 12),
    "H2": ("z", (1, 0, 0), 12, 12),
    "1U1": ("u", (0, 3), 0, 4),
    "1U2": ("u", (0, 3), 4, 4),
    "1D1": ("d", (0, 1), 4, 4),
    "1D2": ("d", (0, 1), 0, 4),
    "1Z1": ("z", (1, 0), 0, 4),
    "1Z2": ("z", (1, 0), 4, 4),
    "1FU": ("u", (0, 2), 0, 4),
    "1FD": ("d", (0, 2), 4, 4),
    "1PU1": ("u", (1, 3), 0, 4),
    "1PD1": ("d", (1, 1), 4, 4),
    "1PU2": ("u", (1, 3), 4, 2),
    "1PD2": ("d", (1, 1), 2, 2),
    "1ZU": ("z", (1, 3), 6, 2),
    "1ZD": ("z", (1, 1), 0, 2),
    "1GU": ("u", (1, 2), 0, 4),
    "1GD": ("d", (1, 2), 4, 4),
}
ORDER = [
    "S 0Z2", "S 0D1", "prep", "S XR2", "S XL2", "S 0U2", "S 1D2", "S H1", "S 0U1", "S XS0", "S H2", "W 0D1", "S XR1",
    "S XL1", "W 0Z2", "S 0PD1", "S 0FD", "W XR2", "S 1U1", "W H1", "S 0Z1", "W XL2", "S YL2", "S YR1", "S 1Z1",
    "W 0U1", "S 0FU", "S 0D2", "W XL1", "S XS1", "S 1U2", "W 1U1", "W H2", "W 0PD1", "S YL1", "prep2", "W 0U2",
    "S 1D1", "S 1Z2", "W XR1", "S YR2", "W YL2", "W 0Z1", "S 0PU1", "S 0PD2", "S 0GD", "S YS0", "S XS3", "S XFR",
    "S 0PU2", "W XS0", "W 1U2", "W 0D2", "S XFL", "S 0ZU", "W YR1", "W 1D2", "W YL1", "S YS1", "E 9", "W 1D1",
    "W 0PU1", "S 0GU", "W 0FD", "E 1", "W YR2", "S YS3", "W 1Z1", "S 0ZD", "W YS1", "S 1PD2", "W 0PU2", "E 13",
    "S 1PU1", "W XS3", "W 0PD2", "W 1Z2", "W YS3", "W XS1", "S YFR", "E 7", "E 5", "W 0FU", "E 11", "S 1PD1", "E 15",
    "S 1ZD", "S 1PU2", "E 0", "S YFL", "E 3", "W 0ZU", "W YS0", "S 1ZU", "W 0GD", "E 4", "E 8", "E 12", "S 1FU",
    "S 1FD", "W XFR", "S XT2", "W XFL", "E 2", "S XU2", "W 0GU", "W 1PD2", "W 0ZD", "P 4 3", "P 13 0", "P 2 11",
    "W XT2", "P 1 8", "P 9 7", "P 12 15", "W XU2", "E 6", "W 1PU1", "W 1PD1", "S 1GU", "W YFR", "S YT2", "S 1GD",
    "W YFL", "W 1ZU", "S YU2", "L 5", "E 10", "W 1PU2", "W YT2", "W 1ZD", "L 10", "W YU2", "E 14", "R 4", "R 1",
    "L 14", "W 1FD", "R 7", "R 3", "R 0", "R 5", "L 6", "W 1FU", "W 1GD", "Q 1", "R 2", "W 1GU", "Q 0",
]
IDS = {}
for _n, _t in TRANSFERS.items():
    IDS[_n] = len(IDS)
    if len(_t[1]) == 3 and _t[2] == 0:
        IDS["m" + _n] = len(IDS)


def kernel(a_in, b_in, mask, order, out, *scratch):
    A = scratch[0:16]
    meta = scratch[16:32]
    (a_loc, dense, b0, b1, inv_v, inv_s, nxt, pos, cnt, ss, rs, ls) = scratch[32:]
    B = (b0, b1)
    row, col = lax.axis_index("row"), lax.axis_index("col")
    y, zl = lax.rem(row, 4), lax.div(row, 4)
    core, zh, x = lax.rem(col, 2), lax.rem(lax.div(col, 2), 2), lax.div(col, 4)

    def at(dx=0, dy=0, dzl=0, dzh=0, dcore=0):
        r = lax.rem(zl + dzl, 2) * 4 + lax.rem(y + dy, 4)
        c = (lax.rem(x + dx, 4) * 2 + lax.rem(zh + dzh, 2)) * 2 + lax.rem(core + dcore, 2)
        return r, c

    up, down, zpart = at(dy=1), at(dy=3), at(dzl=1)
    right, left, hpart, sib = at(dx=1), at(dx=3), at(dzh=1), at(dcore=1)
    peers = (up, down, zpart, right, left, hpart, sib)

    barrier = pltpu.get_barrier_semaphore()
    for p in peers:
        pl.semaphore_signal(barrier, inc=1, device_id=p, device_id_type=MESH)

    local = []
    for k in range(KT):
        local.append(pltpu.make_async_copy(a_in.at[:, :, pl.ds(k * T, T)], a_loc.at[pl.ds(k * ROWT, ROWT)], ls.at[k]))
    for h in (0, 1):
        local.append(pltpu.make_async_copy(b_in.at[:, :, pl.ds(h * H, H)], B[h].at[pl.ds(row * DEPTH, DEPTH)], ls.at[KT + h]))
    for c in local:
        c.start()
    pl.semaphore_wait(barrier, len(peers))

    started = []

    def start(i, src, dst, device):
        c = pltpu.make_async_remote_copy(src, dst, ss.at[i], rs.at[i], device_id=device, device_id_type=MESH)
        c.start()
        started.append(c)

    def arrived(i, ref):
        pltpu.make_async_remote_copy(ref, ref, ss.at[i], rs.at[i], device_id=sib, device_id_type=MESH).wait_recv()

    def slot(dzh, dcore, dx):
        return dzh * 8 + dcore * 4 + dx

    def block(h, dzl, dy, first, count):
        r = lax.rem(zl + dzl, 2) * 4 + lax.rem(y + dy, 4)
        return B[h].at[pl.ds(r * DEPTH + first, count)]

    def send(name):
        way, land, first, count = TRANSFERS[name]
        if len(land) == 2:
            h, (dzl, dy) = int(name[0]), land
            dzl, dy = {"u": (dzl, dy + 1), "d": (dzl, dy + 3), "z": (1 - dzl, dy)}[way]
            dst = block(h, dzl, dy % 4, first, count)
            src = b_in.at[pl.ds(first, count), :, pl.ds(h * H, H)] if (dzl, dy % 4) == (0, 0) else dst
            start(IDS[name], src, dst, {"u": up, "d": down, "z": zpart}[way])
        else:
            dzh, dcore, dx = land
            frm = {"r": (dzh, dcore, dx + 1), "l": (dzh, dcore, dx + 3),
                   "z": (1 - dzh, dcore, dx), "s": (dzh, 1 - dcore, dx)}[way]
            frm, to = slot(frm[0], frm[1], frm[2] % 4), slot(*land)
            device = {"r": right, "l": left, "z": hpart, "s": sib}[way]
            tiles = pl.ds(first, count)
            start(IDS[name], A[frm].at[tiles], A[to].at[tiles], device)
            if first == 0:
                start(IDS["m" + name], meta[frm], meta[to], device)

    def wait(name):
        _, land, first, count = TRANSFERS[name]
        if len(land) == 2:
            arrived(IDS[name], block(int(name[0]), *land, first, count))
        else:
            s = slot(*land)
            arrived(IDS[name], A[s].at[pl.ds(first, count)])
            if first == 0:
                arrived(IDS["m" + name], meta[s])

    def col_of(s):
        dzh, dcore, dx = s // 8, s // 4 % 2, s % 4
        return at(dx=dx, dzh=dzh, dcore=dcore)[1]

    def expand(s):
        base = col_of(s) * KT

        @pl.loop(0, KT)
        def _(j):
            for i in range(ROWT):
                dense[base + j, pl.ds(i * T, T), :] = A[s][meta[s][j * ROWT + i]]

    def add(half, left_tiles, right_tiles):
        rhs = jnp.concatenate(right_tiles, axis=0)
        for m in range(M // CHUNK):
            rows = pl.ds(m * CHUNK, CHUNK)
            lhs = jnp.concatenate([dense[k, rows, :] for k in left_tiles], axis=1)
            out[rows, pl.ds(half * H, H)] += jnp.dot(lhs, rhs, preferred_element_type=jnp.float32)

    def left_part(*slots):
        tiles = [col_of(s) * KT + j for s in slots for j in range(KT)]
        add(0, tiles, [b0[order[k]] for k in tiles])

    def right_part(g, first=0, count=DEPTH):
        r = at(dzl=g // 4, dy=g % 4)[0]
        tiles = [r * DEPTH + first + j for j in range(count)]
        add(1, [inv_s[0, t] for t in tiles], [b1[t] for t in tiles])

    def prepare():
        nxt[KT * ROWT] = 0

        @pl.loop(0, KT * ROWT)
        def _(n):
            t = KT * ROWT - 1 - n
            keep = mask[lax.div(t, ROWT), lax.rem(t, ROWT)]
            nxt[t] = keep * t + (1 - keep) * nxt[t + 1]

        cnt[0] = 0

        @pl.loop(0, KT * ROWT)
        def _(t):
            keep = mask[lax.div(t, ROWT), lax.rem(t, ROWT)]
            meta[0][t] = keep * cnt[t] + (1 - keep) * ZERO
            cnt[t + 1] = cnt[t] + keep

        for k in range(KT):
            local[k].wait()
        pos[0] = nxt[0]

        @pl.loop(0, CAP)
        def _(s):
            A[0][s] = a_loc[pos[s]]
            pos[s + 1] = nxt[pos[s] + 1]

    def prepare_rest():
        lane = lax.broadcasted_iota(jnp.int32, (8, 128), 1)
        inv_v[...] = jnp.zeros((8, 128), jnp.int32)

        @pl.loop(0, 64)
        def _(k):
            apart = lane - order[k]
            inv_v[...] += (k - inv_v[...]) * (1 - jnp.minimum(jnp.maximum(apart, -apart), 1))

        to_s = pltpu.make_async_copy(inv_v, inv_s, ls.at[KT + 2])
        to_s.start()
        for s in range(16):
            A[s][ZERO] = jnp.zeros((T, T), jnp.bfloat16)
        out[...] = jnp.zeros_like(out)
        to_s.wait()
        local[KT].wait()
        local[KT + 1].wait()

    for step in ORDER:
        what, *which = step.split()
        if what == "S":
            send(which[0])
        elif what == "W":
            wait(which[0])
        elif what == "E":
            expand(int(which[0]))
        elif what == "prep":
            prepare()
        elif what == "prep2":
            prepare_rest()
        elif what in "LP":
            left_part(*map(int, which))
        elif what == "R":
            right_part(int(which[0]))
        else:
            right_part(6, int(which[0]) * 4, 4)
    for c in started:
        c.wait_send()


def local_step(amplitudes, integrals, screen_mask, tile_order):
    n = len(IDS)
    scratch = [pltpu.VMEM((CAP + 1, T, T), jnp.bfloat16)] * 16 + [pltpu.SMEM((64,), jnp.int32)] * 16
    scratch += [
        pltpu.VMEM((KT * ROWT, T, T), jnp.bfloat16),
        pltpu.VMEM((64, M, T), jnp.bfloat16),
        pltpu.VMEM((8 * DEPTH, T, H), jnp.bfloat16),
        pltpu.VMEM((8 * DEPTH, T, H), jnp.bfloat16),
        pltpu.VMEM((8, 128), jnp.int32),
        pltpu.SMEM((8, 128), jnp.int32),
        pltpu.SMEM((KT * ROWT + 2,), jnp.int32),
        pltpu.SMEM((KT * ROWT + 2,), jnp.int32),
        pltpu.SMEM((KT * ROWT + 2,), jnp.int32),
        pltpu.SemaphoreType.DMA((n,)),
        pltpu.SemaphoreType.DMA((n,)),
        pltpu.SemaphoreType.DMA((KT + 3,)),
    ]
    anywhere = pl.BlockSpec(memory_space=pl.ANY)
    scalars = pl.BlockSpec(memory_space=pltpu.SMEM)
    return pl.pallas_call(
        kernel,
        out_shape=pltpu.VMEM((M, 2 * H), jnp.float32),
        in_specs=[anywhere, anywhere, scalars, scalars],
        out_specs=pl.BlockSpec(memory_space=pltpu.VMEM),
        scratch_shapes=scratch,
        cost_estimate=pl.CostEstimate(flops=2 * M * 512 * 8192, bytes_accessed=6 << 20, transcendentals=0),
        compiler_params=pltpu.CompilerParams(
            collective_id=0, has_side_effects=True, vmem_limit_bytes=58 << 20
        ),
    )(amplitudes.reshape(ROWT, T, KT * T), integrals.reshape(DEPTH, T, 2 * H), screen_mask.T, tile_order)


def solution(mesh):
    placed = (P("row", "col"), P("row", "col"), P("row", "col"), P())
    return jax.shard_map(
        local_step, mesh=mesh, in_specs=placed, out_specs=P("row", "col"), check_vma=False
    )
```

time: 300 us -> 75.6 us (0.25)
  waiting for transfers between devices: 245 us -> 0 us
  Pallas kernels: 0 us -> 73.8 us
  matrix products: 20.2 us -> 0 us
  between operations: 13.4 us -> 0.01 us
  other arithmetic: 11.2 us -> 0 us
  local copies, waits for them, and re-layouts: 9.57 us -> 1.67 us
    all_gather x2 -> x0, waiting for transfers between devices: 244 us -> none  [the longest x1 152 us: local(): lax.all_gather(screened_tiles, 'col', axis=1, tiled=True)]
    pallas_call x0 -> x1, Pallas kernels: none -> 73.8 us  [local_step(): pl.pallas_call(kernel, out_shape=pltpu.VMEM((M, 2 * H), jnp.float32), in_...]
    dot_general x1 -> x0, matrix products: 20.2 us -> none  [accumulate(): return jnp.dot(left, right, preferred_element_type=jnp.float32)]
    gather x1 -> x0, local copies, waits for them, and re-layouts: 8.91 us -> none  [ordered_rows(): jnp.take(gathered.reshape(all_tiles, TILE_PAIRS, result_cols), tile_order...]
    select_n x2 -> x0, other arithmetic: 7.77 us -> none  [ordered_rows(): jnp.take(gathered.reshape(all_tiles, TILE_PAIRS, result_cols), tile_order...]
  transfers between devices with their start and end apart: 2 -> 0, of which waited for: 2 -> 0; matrix products, arithmetic and copies ran while one was open for 7% -> 0% of each run, Pallas kernels for 0% -> 0%
where the time goes in v3:
time: 75.6 us; the launch traced here: 75.5 us
  Pallas kernels  73.8 us (98%)
  local copies, waits for them, and re-layouts  1.67 us (2%)
    pallas_call x1, Pallas kernels, local_step(): pl.pallas_call(kernel, out_shape=pltpu.VMEM((M, 2 * H), jnp.float32), in_...  73.8 us
    unnamed x1, local copies, waits for them, and re-layouts  1.67 us

profile of v3, /device:TPU:1, one launch (start us, length us, event | category | flops | bytes accessed | tf_op | source)
XLA Modules:
  0.0 75.5 jit_solution(6197960680499555708)
XLA Ops:
  0.0 73.8 %shard_map.46 = f32[1536,512]{1,0:T(8,128)S(1)} custom-call(bf16[12,128,512]{2,1,0:T(8,128)(2,1)} %bitcast.3, bf16[8,128,512]{2,1,0:T(8,128)(2,1)} %bitcast.4, s32[4,12]{1,0:T(4,128)} %bitcast.5, s32[64]{0:T(128)} %order.1), custom_call_target="tpu_custom_call" | custom-call | flops 12884901888 | bytes 6291456 | tf_op jit(solution)/shard_map/pallas_call | solution.py:286
  73.8 1.7 %copy.6 = f32[1536,512]{1,0:T(8,128)} copy(f32[1536,512]{1,0:T(8,128)S(1)} %shard_map.46) | data formatting | bytes 6291456

commit v4 on v3

--- a/solution.py
+++ b/solution.py
@@ -65,26 +65,26 @@
     "1FD": ("d", (0, 2), 4, 4),
     "1PU1": ("u", (1, 3), 0, 4),
     "1PD1": ("d", (1, 1), 4, 4),
-    "1PU2": ("u", (1, 3), 4, 2),
-    "1PD2": ("d", (1, 1), 2, 2),
-    "1ZU": ("z", (1, 3), 6, 2),
-    "1ZD": ("z", (1, 1), 0, 2),
+    "1PU2": ("u", (1, 3), 4, 1),
+    "1PD2": ("d", (1, 1), 3, 1),
+    "1ZU": ("z", (1, 3), 5, 3),
+    "1ZD": ("z", (1, 1), 0, 3),
     "1GU": ("u", (1, 2), 0, 4),
     "1GD": ("d", (1, 2), 4, 4),
 }
 ORDER = [
-    "S 0Z2", "S 0D1", "prep", "S XR2", "S XL2", "S 0U2", "S 1D2", "S H1", "S 0U1", "S XS0", "S H2", "W 0D1", "S XR1",
-    "S XL1", "W 0Z2", "S 0PD1", "S 0FD", "W XR2", "S 1U1", "W H1", "S 0Z1", "W XL2", "S YL2", "S YR1", "S 1Z1",
-    "W 0U1", "S 0FU", "S 0D2", "W XL1", "S XS1", "S 1U2", "W 1U1", "W H2", "W 0PD1", "S YL1", "prep2", "W 0U2",
-    "S 1D1", "S 1Z2", "W XR1", "S YR2", "W YL2", "W 0Z1", "S 0PU1", "S 0PD2", "S 0GD", "S YS0", "S XS3", "S XFR",
-    "S 0PU2", "W XS0", "W 1U2", "W 0D2", "S XFL", "S 0ZU", "W YR1", "W 1D2", "W YL1", "S YS1", "E 9", "W 1D1",
-    "W 0PU1", "S 0GU", "W 0FD", "E 1", "W YR2", "S YS3", "W 1Z1", "S 0ZD", "W YS1", "S 1PD2", "W 0PU2", "E 13",
-    "S 1PU1", "W XS3", "W 0PD2", "W 1Z2", "W YS3", "W XS1", "S YFR", "E 7", "E 5", "W 0FU", "E 11", "S 1PD1", "E 15",
-    "S 1ZD", "S 1PU2", "E 0", "S YFL", "E 3", "W 0ZU", "W YS0", "S 1ZU", "W 0GD", "E 4", "E 8", "E 12", "S 1FU",
-    "S 1FD", "W XFR", "S XT2", "W XFL", "E 2", "S XU2", "W 0GU", "W 1PD2", "W 0ZD", "P 4 3", "P 13 0", "P 2 11",
-    "W XT2", "P 1 8", "P 9 7", "P 12 15", "W XU2", "E 6", "W 1PU1", "W 1PD1", "S 1GU", "W YFR", "S YT2", "S 1GD",
-    "W YFL", "W 1ZU", "S YU2", "L 5", "E 10", "W 1PU2", "W YT2", "W 1ZD", "L 10", "W YU2", "E 14", "R 4", "R 1",
-    "L 14", "W 1FD", "R 7", "R 3", "R 0", "R 5", "L 6", "W 1FU", "W 1GD", "Q 1", "R 2", "W 1GU", "Q 0",
+    "S 0Z2", "S 0U1", "S 0D1", "prep", "S XL1", "S XR1", "S 0U2", "S H1", "S 1D2", "S 0D2", "S 1U2", "S H2", "W 0D1",
+    "S XR2", "S XL2", "W 0Z2", "S 0PU2", "S 1U1", "S 0PD1", "W H1", "W XL1", "S YR1", "W 0U1", "S 0Z1", "prep2",
+    "S YL2", "W XR2", "S XS0", "S 0FD", "W XL2", "W 0PU2", "S 1Z2", "W H2", "S 0FU", "S YL1", "W 0PD1", "S 1D1",
+    "W XR1", "S YR2", "S XS3", "S XFL", "W 0U2", "W 0Z1", "S 0PU1", "S XFR", "S YS0", "S 1Z1", "W YR1", "W 0D2",
+    "S 0PD2", "W 1D1", "W 1D2", "W 1Z2", "S 1PU2", "W 1U2", "W XS0", "S 0GD", "W YR2", "S XS1", "W YL1", "S YFR",
+    "W XS3", "S 0ZD", "W 0PD2", "W 0PU1", "S 0GU", "W YL2", "S 0ZU", "E 0", "S YS3", "S YS1", "W XS1", "S YFL", "E 1",
+    "W 1U1", "E 4", "E 9", "E 11", "W 0FD", "S 1ZD", "W YS1", "E 7", "W 1Z1", "S 1PD2", "E 8", "S 1PU1", "S 1ZU",
+    "S 1PD1", "E 13", "W YS0", "E 3", "W 0GD", "S 1FD", "E 5", "W 0FU", "W XFL", "S XU2", "W XFR", "S XT2", "E 12",
+    "S 1FU", "W 1PU2", "E 2", "W YS3", "W 1PD2", "W 0ZD", "E 15", "W 0GU", "W XT2", "W XU2", "E 6", "W 0ZU",
+    "L 3 5 13 15", "L 12 2 11 7", "L 1 4 6 0", "L 9", "W 1PD1", "S 1GD", "W 1PU1", "W 1ZD", "W YFL", "W YFR", "S YU2",
+    "S 1GU", "S YT2", "E 10", "L 8 10", "W YU2", "W YT2", "E 14", "R 6 7 10 11", "R 8 9", "W 1ZU", "W 1FU", "W 1FD",
+    "R 4 5 0 1", "R 14 15 2 3", "L 14", "W 1GD", "R 13", "W 1GU", "R 12",
 ]
 IDS = {}
 for _n, _t in TRANSFERS.items():
@@ -122,6 +122,22 @@
         local.append(pltpu.make_async_copy(b_in.at[:, :, pl.ds(h * H, H)], B[h].at[pl.ds(row * DEPTH, DEPTH)], ls.at[KT + h]))
     for c in local:
         c.start()
+    nxt[KT * ROWT] = 0
+
+    @pl.loop(0, KT * ROWT)
+    def _(n):
+        t = KT * ROWT - 1 - n
+        keep = mask[lax.div(t, ROWT), lax.rem(t, ROWT)]
+        nxt[t] = keep * t + (1 - keep) * nxt[t + 1]
+
+    cnt[0] = 0
+
+    @pl.loop(0, KT * ROWT)
+    def _(t):
+        keep = mask[lax.div(t, ROWT), lax.rem(t, ROWT)]
+        meta[0][t] = keep * cnt[t] + (1 - keep) * ZERO
+        cnt[t + 1] = cnt[t] + keep
+
     pl.semaphore_wait(barrier, len(peers))
 
     started = []
@@ -193,28 +209,11 @@
         tiles = [col_of(s) * KT + j for s in slots for j in range(KT)]
         add(0, tiles, [b0[order[k]] for k in tiles])
 
-    def right_part(g, first=0, count=DEPTH):
-        r = at(dzl=g // 4, dy=g % 4)[0]
-        tiles = [r * DEPTH + first + j for j in range(count)]
+    def right_part(*quads):
+        tiles = [at(dzl=q // 8, dy=q // 2 % 4)[0] * DEPTH + q % 2 * 4 + j for q in quads for j in range(4)]
         add(1, [inv_s[0, t] for t in tiles], [b1[t] for t in tiles])
 
     def prepare():
-        nxt[KT * ROWT] = 0
-
-        @pl.loop(0, KT * ROWT)
-        def _(n):
-            t = KT * ROWT - 1 - n
-            keep = mask[lax.div(t, ROWT), lax.rem(t, ROWT)]
-            nxt[t] = keep * t + (1 - keep) * nxt[t + 1]
-
-        cnt[0] = 0
-
-        @pl.loop(0, KT * ROWT)
-        def _(t):
-            keep = mask[lax.div(t, ROWT), lax.rem(t, ROWT)]
-            meta[0][t] = keep * cnt[t] + (1 - keep) * ZERO
-            cnt[t + 1] = cnt[t] + keep
-
         for k in range(KT):
             local[k].wait()
         pos[0] = nxt[0]
@@ -254,12 +253,10 @@
             prepare()
         elif what == "prep2":
             prepare_rest()
-        elif what in "LP":
+        elif what == "L":
             left_part(*map(int, which))
-        elif what == "R":
-            right_part(int(which[0]))
         else:
-            right_part(6, int(which[0]) * 4, 4)
+            right_part(*map(int, which))
     for c in started:
         c.wait_send()
 

time: 75.6 us -> 73.8 us (0.976)
  Pallas kernels: 73.8 us -> 72 us
    pallas_call x1, Pallas kernels: 73.8 us -> 72 us  [local_step(): pl.pallas_call(kernel, out_shape=pltpu.VMEM((M, 2 * H), jnp.float32), in_...]
where the time goes in v4:
time: 73.8 us; the launch traced here: 73.7 us
  Pallas kernels  72 us (98%)
  local copies, waits for them, and re-layouts  1.67 us (2%)
    pallas_call x1, Pallas kernels, local_step(): pl.pallas_call(kernel, out_shape=pltpu.VMEM((M, 2 * H), jnp.float32), in_...  72 us
    unnamed x1, local copies, waits for them, and re-layouts  1.67 us

profile of v4, /device:TPU:1, one launch (start us, length us, event | category | flops | bytes accessed | tf_op | source)
XLA Modules:
  0.0 73.7 jit_solution(17376908540435475212)
XLA Ops:
  0.0 72.0 %shard_map.46 = f32[1536,512]{1,0:T(8,128)S(1)} custom-call(bf16[12,128,512]{2,1,0:T(8,128)(2,1)} %bitcast.3, bf16[8,128,512]{2,1,0:T(8,128)(2,1)} %bitcast.4, s32[4,12]{1,0:T(4,128)} %bitcast.5, s32[64]{0:T(128)} %order.1), custom_call_target="tpu_custom_call" | custom-call | flops 12884901888 | bytes 6291456 | tf_op jit(solution)/shard_map/pallas_call | solution.py:283
  72.0 1.7 %copy.6 = f32[1536,512]{1,0:T(8,128)} copy(f32[1536,512]{1,0:T(8,128)S(1)} %shard_map.46) | data formatting | bytes 6291456

commit v5 on v4

--- a/solution.py
+++ b/solution.py
@@ -11,6 +11,7 @@
 M = ROWT * T
 DEPTH = 8
 H = 256
+LATE = (10, 14)
 ZERO = CAP
 CHUNK = 768
 
@@ -65,27 +66,26 @@
     "1FD": ("d", (0, 2), 4, 4),
     "1PU1": ("u", (1, 3), 0, 4),
     "1PD1": ("d", (1, 1), 4, 4),
-    "1PU2": ("u", (1, 3), 4, 1),
-    "1PD2": ("d", (1, 1), 3, 1),
-    "1ZU": ("z", (1, 3), 5, 3),
-    "1ZD": ("z", (1, 1), 0, 3),
+    "1ZU": ("z", (1, 3), 4, 4),
+    "1ZD": ("z", (1, 1), 0, 4),
     "1GU": ("u", (1, 2), 0, 4),
     "1GD": ("d", (1, 2), 4, 4),
 }
 ORDER = [
-    "S 0Z2", "S 0U1", "S 0D1", "prep", "S XL1", "S XR1", "S 0U2", "S H1", "S 1D2", "S 0D2", "S 1U2", "S H2", "W 0D1",
-    "S XR2", "S XL2", "W 0Z2", "S 0PU2", "S 1U1", "S 0PD1", "W H1", "W XL1", "S YR1", "W 0U1", "S 0Z1", "prep2",
-    "S YL2", "W XR2", "S XS0", "S 0FD", "W XL2", "W 0PU2", "S 1Z2", "W H2", "S 0FU", "S YL1", "W 0PD1", "S 1D1",
-    "W XR1", "S YR2", "S XS3", "S XFL", "W 0U2", "W 0Z1", "S 0PU1", "S XFR", "S YS0", "S 1Z1", "W YR1", "W 0D2",
-    "S 0PD2", "W 1D1", "W 1D2", "W 1Z2", "S 1PU2", "W 1U2", "W XS0", "S 0GD", "W YR2", "S XS1", "W YL1", "S YFR",
-    "W XS3", "S 0ZD", "W 0PD2", "W 0PU1", "S 0GU", "W YL2", "S 0ZU", "E 0", "S YS3", "S YS1", "W XS1", "S YFL", "E 1",
-    "W 1U1", "E 4", "E 9", "E 11", "W 0FD", "S 1ZD", "W YS1", "E 7", "W 1Z1", "S 1PD2", "E 8", "S 1PU1", "S 1ZU",
-    "S 1PD1", "E 13", "W YS0", "E 3", "W 0GD", "S 1FD", "E 5", "W 0FU", "W XFL", "S XU2", "W XFR", "S XT2", "E 12",
-    "S 1FU", "W 1PU2", "E 2", "W YS3", "W 1PD2", "W 0ZD", "E 15", "W 0GU", "W XT2", "W XU2", "E 6", "W 0ZU",
-    "L 3 5 13 15", "L 12 2 11 7", "L 1 4 6 0", "L 9", "W 1PD1", "S 1GD", "W 1PU1", "W 1ZD", "W YFL", "W YFR", "S YU2",
-    "S 1GU", "S YT2", "E 10", "L 8 10", "W YU2", "W YT2", "E 14", "R 6 7 10 11", "R 8 9", "W 1ZU", "W 1FU", "W 1FD",
-    "R 4 5 0 1", "R 14 15 2 3", "L 14", "W 1GD", "R 13", "W 1GU", "R 12",
+    "S 0Z1", "S 0U1", "S 0D1", "prep", "S XL1", "S XR1", "S XS0", "S 0U2", "S 0Z2", "S H1", "W XS0", "S 1D1", "S 1U1",
+    "W 0Z1", "S H2", "S XR2", "S 0PD2", "S XL2", "W 0D1", "S 0D2", "W 0Z2", "S 1Z1", "S 0PD1", "S 1D2", "W 0U2",
+    "prep2", "S 1Z2", "S 0PU2", "W XR1", "W XL1", "W 0U1", "W 1D1", "S 1U2", "S XFR", "S XFL", "W XL2", "S XS1",
+    "S 0ZU", "W XR2", "S 0PU1", "S XS3", "W XS1", "E 0", "W H1", "S YL2", "S 0FU", "S YR1", "W XS3", "W 0D2",
+    "W 0PD1", "W 0PD2", "W 0PU2", "W XFL", "S XU2", "S 0FD", "S 0GD", "W XFR", "S XT2", "W H2", "S YS0", "S 0ZD",
+    "S YL1", "E 3", "S YR2", "W 0PU1", "W 1U1", "E 8", "S 0GU", "W 1Z1", "W YR1", "W XU2", "S 1PU1", "W 1D2", "W YS0",
+    "E 12", "W 0FD", "W XT2", "E 6", "W YL2", "S 1ZD", "E 7", "S 1FU", "E 5", "S YFR", "W 1Z2", "S 1PD1", "S 1FD",
+    "E 2", "W 0GU", "W 0FU", "W YL1", "S YFL", "S YS1", "W 1U2", "E 9", "W YR2", "E 11", "S YS3", "S 1ZU", "E 1",
+    "E 4", "W 0GD", "W 0ZU", "W 0ZD", "L 0.6.11.3", "L 7.2.9.12", "W 1PD1", "S 1GD", "W YS1", "E 13", "W YS3",
+    "W 1PU1", "E 15", "S 1GU", "L 4.15.5.13", "R 6.7.0.1", "W YFR", "S YT2", "R 8.9.2.3", "W 1ZD", "W 1FU", "W YT2",
+    "W 1FD", "W YFL", "S YU2", "R 10.11.4.5", "W YU2", "W 1ZU", "R 14.15", "E 10", "E 14", "L 8.1.14.10", "W 1GD",
+    "W 1GU", "R 12.16.17.13",
 ]
+FIRST = [step[0] for step in ORDER].index("L")
 IDS = {}
 for _n, _t in TRANSFERS.items():
     IDS[_n] = len(IDS)
@@ -96,7 +96,7 @@
 def kernel(a_in, b_in, mask, order, out, *scratch):
     A = scratch[0:16]
     meta = scratch[16:32]
-    (a_loc, dense, b0, b1, inv_v, inv_s, nxt, pos, cnt, ss, rs, ls) = scratch[32:]
+    (a_loc, dense, late, b0, b1, inv_v, inv_s, nxt, pos, cnt, ss, rs, ls) = scratch[32:]
     B = (b0, b1)
     row, col = lax.axis_index("row"), lax.axis_index("col")
     y, zl = lax.rem(row, 4), lax.div(row, 4)
@@ -120,7 +120,7 @@
         local.append(pltpu.make_async_copy(a_in.at[:, :, pl.ds(k * T, T)], a_loc.at[pl.ds(k * ROWT, ROWT)], ls.at[k]))
     for h in (0, 1):
         local.append(pltpu.make_async_copy(b_in.at[:, :, pl.ds(h * H, H)], B[h].at[pl.ds(row * DEPTH, DEPTH)], ls.at[KT + h]))
-    for c in local:
+    for c in local[KT:] + local[:KT]:
         c.start()
     nxt[KT * ROWT] = 0
 
@@ -138,14 +138,22 @@
         meta[0][t] = keep * cnt[t] + (1 - keep) * ZERO
         cnt[t + 1] = cnt[t] + keep
 
+    local[KT].wait()
+    local[KT + 1].wait()
     pl.semaphore_wait(barrier, len(peers))
 
-    started = []
+    started = {}
 
     def start(i, src, dst, device):
         c = pltpu.make_async_remote_copy(src, dst, ss.at[i], rs.at[i], device_id=device, device_id_type=MESH)
         c.start()
-        started.append(c)
+        started[i] = c
+
+    def drain(names):
+        for n in names:
+            for i in (IDS[n], IDS.get("m" + n)):
+                if i in started:
+                    started.pop(i).wait_send()
 
     def arrived(i, ref):
         pltpu.make_async_remote_copy(ref, ref, ss.at[i], rs.at[i], device_id=sib, device_id_type=MESH).wait_recv()
@@ -163,8 +171,7 @@
             h, (dzl, dy) = int(name[0]), land
             dzl, dy = {"u": (dzl, dy + 1), "d": (dzl, dy + 3), "z": (1 - dzl, dy)}[way]
             dst = block(h, dzl, dy % 4, first, count)
-            src = b_in.at[pl.ds(first, count), :, pl.ds(h * H, H)] if (dzl, dy % 4) == (0, 0) else dst
-            start(IDS[name], src, dst, {"u": up, "d": down, "z": zpart}[way])
+            start(IDS[name], dst, dst, {"u": up, "d": down, "z": zpart}[way])
         else:
             dzh, dcore, dx = land
             frm = {"r": (dzh, dcore, dx + 1), "l": (dzh, dcore, dx + 3),
@@ -190,28 +197,45 @@
         dzh, dcore, dx = s // 8, s // 4 % 2, s % 4
         return at(dx=dx, dzh=dzh, dcore=dcore)[1]
 
+    def place(s):
+        if s in LATE:
+            return late.at[pl.ds(LATE.index(s) * KT, KT)]
+        return dense.at[pl.ds(col_of(s) * KT, KT)]
+
     def expand(s):
-        base = col_of(s) * KT
+        to = place(s)
 
         @pl.loop(0, KT)
         def _(j):
             for i in range(ROWT):
-                dense[base + j, pl.ds(i * T, T), :] = A[s][meta[s][j * ROWT + i]]
+                to[j, pl.ds(i * T, T), :] = A[s][meta[s][j * ROWT + i]]
 
     def add(half, left_tiles, right_tiles):
         rhs = jnp.concatenate(right_tiles, axis=0)
         for m in range(M // CHUNK):
             rows = pl.ds(m * CHUNK, CHUNK)
-            lhs = jnp.concatenate([dense[k, rows, :] for k in left_tiles], axis=1)
+            lhs = jnp.concatenate([ref[k, rows, :] for ref, k in left_tiles], axis=1)
             out[rows, pl.ds(half * H, H)] += jnp.dot(lhs, rhs, preferred_element_type=jnp.float32)
 
-    def left_part(*slots):
-        tiles = [col_of(s) * KT + j for s in slots for j in range(KT)]
-        add(0, tiles, [b0[order[k]] for k in tiles])
-
-    def right_part(*quads):
-        tiles = [at(dzl=q // 8, dy=q // 2 % 4)[0] * DEPTH + q % 2 * 4 + j for q in quads for j in range(4)]
-        add(1, [inv_s[0, t] for t in tiles], [b1[t] for t in tiles])
+    def panel(s, b):
+        c = col_of(s) * KT
+        return [(place(s), j) for j in range(KT)], [b[order[c + j]] for j in range(KT)]
+
+    def left_part(slots):
+        parts = [panel(s, b0) for s in slots]
+        add(0, sum((p[0] for p in parts), []), sum((p[1] for p in parts), []))
+
+    def right_part(quads):
+        lefts, rights = [], []
+        for q in quads:
+            if q >= 16:
+                p = panel(LATE[q - 16], b1)
+                lefts, rights = lefts + p[0], rights + p[1]
+                continue
+            tile = at(dzl=q // 8, dy=q // 2 % 4)[0] * DEPTH + q % 2 * 4
+            lefts += [(dense, inv_s[0, tile + j]) for j in range(4)]
+            rights += [b1[tile + j] for j in range(4)]
+        add(1, lefts, rights)
 
     def prepare():
         for k in range(KT):
@@ -237,16 +261,21 @@
         for s in range(16):
             A[s][ZERO] = jnp.zeros((T, T), jnp.bfloat16)
         out[...] = jnp.zeros_like(out)
+        for s in LATE:
+            dense[pl.ds(col_of(s) * KT, KT)] = jnp.zeros((KT, M, T), jnp.bfloat16)
         to_s.wait()
-        local[KT].wait()
-        local[KT + 1].wait()
-
-    for step in ORDER:
+
+    waited = []
+    last = [i for i, step in enumerate(ORDER) if step[0] == "W"][-1]
+    for i, step in enumerate(ORDER):
         what, *which = step.split()
         if what == "S":
             send(which[0])
         elif what == "W":
+            if i < FIRST or i == last:
+                drain(waited[:-4])
             wait(which[0])
+            waited.append(which[0])
         elif what == "E":
             expand(int(which[0]))
         elif what == "prep":
@@ -254,11 +283,10 @@
         elif what == "prep2":
             prepare_rest()
         elif what == "L":
-            left_part(*map(int, which))
+            left_part([int(n) for n in which[0].split(".")])
         else:
-            right_part(*map(int, which))
-    for c in started:
-        c.wait_send()
+            right_part([int(n) for n in which[0].split(".")])
+    drain(waited)
 
 
 def local_step(amplitudes, integrals, screen_mask, tile_order):
@@ -267,6 +295,7 @@
     scratch += [
         pltpu.VMEM((KT * ROWT, T, T), jnp.bfloat16),
         pltpu.VMEM((64, M, T), jnp.bfloat16),
+        pltpu.VMEM((2 * KT, M, T), jnp.bfloat16),
         pltpu.VMEM((8 * DEPTH, T, H), jnp.bfloat16),
         pltpu.VMEM((8 * DEPTH, T, H), jnp.bfloat16),
         pltpu.VMEM((8, 128), jnp.int32),

time: 73.8 us -> 73.3 us (level)
  no operation moved by 1% of the time
where the time goes in v5:
time: 73.3 us; the launch traced here: 73.2 us
  Pallas kernels  71.5 us (98%)
  local copies, waits for them, and re-layouts  1.67 us (2%)
    pallas_call x1, Pallas kernels, local_step(): pl.pallas_call(kernel, out_shape=pltpu.VMEM((M, 2 * H), jnp.float32), in_...  71.5 us
    unnamed x1, local copies, waits for them, and re-layouts  1.67 us

profile of v5, /device:TPU:1, one launch (start us, length us, event | category | flops | bytes accessed | tf_op | source)
XLA Modules:
  0.0 73.2 jit_solution(2029379649617057957)
XLA Ops:
  0.0 71.5 %shard_map.46 = f32[1536,512]{1,0:T(8,128)S(1)} custom-call(bf16[12,128,512]{2,1,0:T(8,128)(2,1)} %bitcast.3, bf16[8,128,512]{2,1,0:T(8,128)(2,1)} %bitcast.4, s32[4,12]{1,0:T(4,128)} %bitcast.5, s32[64]{0:T(128)} %order.1), custom_call_target="tpu_custom_call" | custom-call | flops 12884901888 | bytes 6291456 | tf_op jit(solution)/shard_map/pallas_call | solution.py:312
  71.5 1.7 %copy.6 = f32[1536,512]{1,0:T(8,128)} copy(f32[1536,512]{1,0:T(8,128)S(1)} %shard_map.46) | data formatting | bytes 6291456
